TPU v7x, 32 devices: a whole 2x2x4 slice. The times are simulated.
32 devices in a mesh: pair: 8 (over y, x, core), rep: 4 (over z).
Axes of the slice: x: 2, y: 2, z: 4, core: 2. Of those that a mesh axis runs over, the one named last changes fastest.
Arguments:
- amplitudes: bfloat16 [256, 4096], P('pair', 'rep'), may hold values from -6 to 6
- integrals: bfloat16 [4096, 4096], P('rep', 'pair'), may hold values from -0.25 to 0.25
- vir_offsets: int32 [9], replicated, may hold values from 0 to 4096, as said below
- vir_energy: float32 [4096], replicated, may hold values from 0.5 to 4
- occ_energy: float32 [256], P(('pair', 'rep')), may hold values from -3 to -0.3
Outputs:
- update: float32 [256, 4096], P(('pair', 'rep'))
Inputs may be any that keep to these rules, and one draw needn't show every extreme that they name: Entries never fall, the first is 0 and the last 4096; irrep g holds the virtual pairs vir_offsets[g] to vir_offsets[g + 1] - 1, and no irrep is empty.
All inputs are finite; a program needn't handle non-finite values.
Results may differ from a plain program's by a relative error of at most 0.0003.
Values may be sent and summed in bfloat16 or wider, within the bound.
A program may use at most 192 MiB of HBM per device.

v0:
```python
import jax
import jax.numpy as jnp
from jax import lax
from jax.sharding import PartitionSpec as P


def irrep_of(indices, vir_offsets):
    return jnp.sum((indices[:, None] >= vir_offsets[None, 1:8]).astype(jnp.int32), axis=1)


def per_device(amplitudes, integrals, vir_offsets, vir_energy, occ_energy):
    slice_rows = integrals.shape[0]
    tile_cols = integrals.shape[1]
    own_rows = lax.iota(jnp.int32, slice_rows) + lax.axis_index("rep") * slice_rows
    row_irrep = irrep_of(own_rows, vir_offsets)
    column_ids = lax.iota(jnp.int32, tile_cols) + lax.axis_index("pair") * tile_cols
    same_irrep = row_irrep[:, None] == irrep_of(column_ids, vir_offsets)[None, :]
    masked = jnp.where(same_irrep, integrals, jnp.zeros_like(integrals))
    partial_value = jnp.dot(
        lax.all_gather(amplitudes, "pair", axis=0, tiled=True),
        masked,
        preferred_element_type=jnp.float32,
    )
    regrouped = lax.all_to_all(partial_value, "pair", split_axis=0, concat_axis=1, tiled=True)
    ladder = lax.psum_scatter(regrouped, "rep", scatter_dimension=0, tiled=True)
    return ladder / (vir_energy[None, :] - occ_energy[:, None])


def solution(mesh):
    placed = (P("pair", "rep"), P("rep", "pair"), P(), P(), P(("pair", "rep")))
    return jax.shard_map(
        per_device, mesh=mesh, in_specs=placed, out_specs=P(("pair", "rep"), None), check_vma=False
    )
```

profile of v0, /device:TPU:0, one launch (start us, length us, event | category | flops | bytes accessed | tf_op | source)
XLA Modules:
  0.0 63.6 jit_solution(15838453354437609126)
XLA Ops:
  6.5 0.0 reduce-scatter.2.cloned.1.call-start
  6.5 0.7 %slice.4 = s32[7]{0:T(128)S(1)} slice(s32[9]{0:T(128)} %param.7), slice={[1:8]} | slice | bytes 56 | tf_op jit(solution)/shard_map/slice | solution.py:8
  7.3 0.1 convert_reduce_fusion.1
  7.4 0.1 convert_reduce_fusion
  7.4 11.6 %all_gather.3 = bf16[256,1024]{1,0:T(8,128)(2,1)S(1)} all-gather(bf16[32,1024]{1,0:T(8,128)(2,1)} %param.5), channel_id=1, replica_groups=mesh['pair'=8,'rep'=4] {'pair'}, dimensions={0}, use_global_device_ids=true | all-gather | bytes 589824 | tf_op jit(solution)/shard_map/all_gather | solution.py:20
  19.0 1.8 %fusion = f32[512,256]{0,1:T(8,128)S(1)} fusion(bf16[256,1024]{1,0:T(8,128)(2,1)S(1)} %all_gather.3, bf16[1024,512]{1,0:T(8,128)(2,1)} %param.6, s32[512]{0:T(512)S(1)} %convert_reduce_fusion.1, s32[1024]{0:T(1024)S(1)} %convert_reduce_fusion), kind=kOutput, calls=%fused_computation.1 | convolution fusion | flops 269484032 | bytes 2103296 | tf_op jit(solution)/shard_map/dot_general | solution.py:19
  20.8 12.3 %all_to_all.19 = f32[8,32,512]{2,1,0:T(8,128)S(1)} all-to-all(f32[8,32,512]{2,1,0:T(8,128)S(1)} %bitcast.9), channel_id=1, replica_groups=mesh['pair'=8,'rep'=4] {'pair'}, dimensions={0} | all-to-all | bytes 1048576 | tf_op jit(solution)/shard_map/all_to_all | solution.py:24
  33.1 0.0 copy-start
  33.1 0.0 copy-start.1
  33.1 0.8 %copy.8 = f32[8,4,8,512]{3,2,0,1:T(8,128)} copy(f32[8,4,8,512]{3,2,1,0:T(8,128)S(1)} %bitcast.8) | data formatting | bytes 1048576 | tf_op jit(solution)/shard_map/all_to_all | solution.py:24
  34.0 0.0 reduce-scatter.2.cloned.1.call-update
  34.0 21.2 %reduce-scatter.2.cloned.1.call-done = f32[8,4096]{1,0:T(8,128)} async-done(((f32[32,4096]{1,0:T(8,128)}), f32[8,4096]{1,0:T(8,128)}) %reduce-scatter.2.cloned.1.call-update) | async-done | bytes 131088 | tf_op jit(solution)/shard_map/reduce_scatter | solution.py:25
  55.1 0.0 copy-done
  55.1 0.0 copy-done.1
  55.1 1.7 %subtract_divide_fusion = f32[8,4096]{1,0:T(8,128)} fusion(f32[8,4096]{1,0:T(8,128)} %reduce-scatter.2.cloned.1.call-done, f32[8]{0:T(128)S(1)} %copy-done.1, f32[4096]{0:T(1024)S(1)} %copy-done), kind=kLoop, calls=%fused_computation.5 | loop fusion | flops 65536 | bytes 278560 | tf_op jit(solution)/shard_map/div | solution.py:26
  (2 shorter events, 0.0 us)
Async XLA Ops:
  6.5 48.6 %reduce-scatter.2.cloned.1.call-start = ((), (), s32[]{:S(2)}) async-start(), calls=%async_computation.2 | async-start | bytes 655360 | tf_op jit(solution)/shard_map/reduce_scatter | solution.py:25
  33.1 22.0 %copy-start = (f32[4096]{0:T(1024)S(1)}, f32[4096]{0:T(1024)}, u32[]{:S(2)}) copy-start(f32[4096]{0:T(1024)} %param.8) | copy-start | bytes 49156
  33.1 22.0 %copy-start.1 = (f32[8]{0:T(128)S(1)}, f32[8]{0:T(128)}, u32[]{:S(2)}) copy-start(f32[8]{0:T(128)} %param.9) | copy-start | bytes 100
Sparse Core Ops, SparseCore 0:
  34.1 20.9 reduce-scatter.1
where the time goes:
time: 63.9 us; the launch traced here: 63.6 us
  blocking collectives  23.9 us (37%)
  waiting for transfers between devices  21.2 us (33%)
  between operations  13.4 us (21%)
  other arithmetic  1.82 us (3%)
  matrix products  1.78 us (3%)
  local copies, waits for them, and re-layouts  1.56 us (2%)
    reduce_scatter x1, waiting for transfers between devices, per_device(): ladder = lax.psum_scatter(regrouped, 'rep', scatter_dimension=0, tiled=True)  21.2 us
    all_to_all x1, blocking collectives, per_device(): lax.all_to_all(partial_value, 'pair', split_axis=0, concat_axis=1, tiled=...  12.3 us
    all_gather x1, blocking collectives, per_device(): lax.all_gather(amplitudes, 'pair', axis=0, tiled=True)  11.6 us
    dot_general x1, matrix products, per_device(): jnp.dot(lax.all_gather(amplitudes, 'pair', axis=0, tiled=True), masked, p...  1.78 us
    div x1, other arithmetic, per_device(): return ladder / (vir_energy[None, :] - occ_energy[:, None])  1.65 us
  transfers between devices with their start and end apart: 1, of which 1 were waited for; matrix products, arithmetic and copies ran while one was open for 0% of the time, Pallas kernels for 0%

commit v1 on v0

v1 whole, which is shorter than its diff:
```python
import functools
import math

import jax
import jax.numpy as jnp
from jax import lax
from jax.experimental import pallas as pl
from jax.experimental.pallas import tpu as pltpu
from jax.sharding import PartitionSpec as P

MESH = pl.DeviceIdType.MESH


def kernel(n, R, amp_ref, int_ref, off_ref, ve_ref, occ_ref, out_ref,
           amp_all, masked, part, rs_buf, red, fin,
           load_sem, ag_send, ag_recv, rs_send, rs_recv, fin_send, fin_recv):
    p = lax.axis_index("pair")
    r = lax.axis_index("rep")
    rows, K = amp_ref.shape
    cols = int_ref.shape[1]
    m = rows // R
    chips = n // 2
    X = math.isqrt(chips)
    Y = chips // X
    core = p % 2
    cx = (p // 2) % X
    cy = p // 2 // X

    def peer(t, sign):
        s = t + 1
        o = s // 2
        x = (cx + X + sign * (o % X)) % X
        y = (cy + 2 * Y + sign * (o // X)) % Y
        return (y * X + x) * 2 + (core + (s + 1) % 2) % 2

    barrier = pltpu.get_barrier_semaphore()

    def greet(i, c):
        pl.semaphore_signal(barrier, inc=1, device_id=((p + i) % n, r), device_id_type=MESH)
        return c
    lax.fori_loop(1, n, greet, 0)
    for i in range(1, R):
        pl.semaphore_signal(barrier, inc=1, device_id=(p, (r + i) % R), device_id_type=MESH)

    load = pltpu.make_async_copy(int_ref, masked, load_sem)
    load.start()
    amp_all[p] = amp_ref[...]

    col = lax.broadcasted_iota(jnp.int32, (8, cols), 1) + p * cols
    lo = jnp.zeros((8, cols), jnp.int32)
    hi = jnp.full((8, cols), n * cols, jnp.int32)
    for g in range(1, 8):
        edge = off_ref[g]
        lo = jnp.where(col >= edge, jnp.maximum(lo, edge), lo)
        hi = jnp.where(col < edge, jnp.minimum(hi, edge), hi)
    lo = lo[:1] - r * K
    hi = hi[:1] - r * K
    load.wait()

    step = 128

    def mask_rows(i, c):
        at = pl.ds(pl.multiple_of(i * step, step), step)
        row = lax.broadcasted_iota(jnp.int32, (step, cols), 0) + i * step
        block = masked[at, :]
        keep = (row >= lo) & (row < hi)
        masked[at, :] = jnp.where(keep, block, jnp.zeros_like(block))
        return c
    lax.fori_loop(0, K // step, mask_rows, 0)

    pl.semaphore_wait(barrier, n - 1 + R - 1)

    def gather_copy(to):
        return pltpu.make_async_remote_copy(
            src_ref=amp_ref, dst_ref=amp_all.at[p], send_sem=ag_send.at[to], recv_sem=ag_recv.at[p],
            device_id=(to, r), device_id_type=MESH)

    def gather_from(q):
        return pltpu.make_async_remote_copy(
            src_ref=amp_ref, dst_ref=amp_all.at[q], send_sem=ag_send.at[q], recv_sem=ag_recv.at[q],
            device_id=(q, r), device_id_type=MESH)

    def send_amp(t, c):
        gather_copy(peer(t, -1)).start()
        return c
    lax.fori_loop(1, n, send_amp, 0)

    def sum_copy(q, to, slot):
        return pltpu.make_async_remote_copy(
            src_ref=part.at[q, to], dst_ref=rs_buf.at[q, slot], send_sem=rs_send.at[q, to],
            recv_sem=rs_recv.at[q, slot], device_id=(p, to), device_id_type=MESH)

    def multiply(t, c):
        q = peer(t, 1)

        @pl.when(t > 0)
        def _():
            gather_from(q).wait_recv()
        d = jnp.dot(amp_all[q], masked[...], preferred_element_type=jnp.float32)
        for k in range(R):
            part[q, k] = d[k * m:(k + 1) * m]
        for i in range(1, R):
            sum_copy(q, (r + i) % R, r).start()
        return c
    lax.fori_loop(0, n, multiply, 0)

    def final_copy(to, slot):
        return pltpu.make_async_remote_copy(
            src_ref=red.at[to], dst_ref=fin.at[slot], send_sem=fin_send.at[to], recv_sem=fin_recv.at[slot],
            device_id=(to, r), device_id_type=MESH)

    def reduce(t, c):
        q = peer(t, 1)
        total = part[q, r]
        for i in range(1, R):
            k = (r + i) % R
            sum_copy(q, k, k).wait_recv()
            total = total + rs_buf[q, k]

        @pl.when(t == 0)
        def _():
            fin[p] = total

        @pl.when(t > 0)
        def _():
            red[q] = total
            final_copy(q, p).start()
        return c
    lax.fori_loop(0, n, reduce, 0)

    which = lax.broadcasted_iota(jnp.int32, (m, cols), 0)
    occ = jnp.zeros((m, cols), jnp.float32)
    for i in range(m):
        occ = jnp.where(which == i, occ_ref[i], occ)

    def finish(t, c):
        q = peer(t, 1)

        @pl.when(t > 0)
        def _():
            final_copy(q, q).wait_recv()
        at = pl.ds(pl.multiple_of(q * cols, cols), cols)
        out_ref[:, at] = fin[q] / (ve_ref[:, at] - occ)
        return c
    lax.fori_loop(0, n, finish, 0)

    def drain(t, c):
        q = peer(t, 1)

        @pl.when(t > 0)
        def _():
            gather_from(q).wait_send()
            final_copy(q, p).wait_send()
        for i in range(1, R):
            sum_copy(q, (r + i) % R, r).wait_send()
        return c
    lax.fori_loop(0, n, drain, 0)


def per_device(n, R, amplitudes, integrals, vir_offsets, vir_energy, occ_energy):
    rows, K = amplitudes.shape
    cols = integrals.shape[1]
    m = rows // R
    vmem = pl.BlockSpec(memory_space=pltpu.VMEM)
    smem = pl.BlockSpec(memory_space=pltpu.SMEM)
    dma = pltpu.SemaphoreType.DMA
    return pl.pallas_call(
        functools.partial(kernel, n, R),
        out_shape=jax.ShapeDtypeStruct((m, n * cols), jnp.float32),
        in_specs=[vmem, pl.BlockSpec(memory_space=pl.ANY), smem, vmem, smem],
        out_specs=vmem,
        scratch_shapes=[
            pltpu.VMEM((n, rows, K), jnp.bfloat16),
            pltpu.VMEM((K, cols), jnp.bfloat16),
            pltpu.VMEM((n, R, m, cols), jnp.float32),
            pltpu.VMEM((n, R, m, cols), jnp.float32),
            pltpu.VMEM((n, m, cols), jnp.float32),
            pltpu.VMEM((n, m, cols), jnp.float32),
            dma, dma((n,)), dma((n,)), dma((n, R)), dma((n, R)), dma((n,)), dma((n,)),
        ],
        compiler_params=pltpu.CompilerParams(
            collective_id=0, has_side_effects=True, vmem_limit_bytes=40 * 1024 * 1024),
        cost_estimate=pl.CostEstimate(
            flops=2 * n * rows * K * cols, bytes_accessed=2 * K * cols, transcendentals=0),
    )(amplitudes, integrals, vir_offsets, vir_energy.reshape(1, -1), occ_energy)


def solution(mesh):
    placed = (P("pair", "rep"), P("rep", "pair"), P(), P(), P(("pair", "rep")))
    return jax.shard_map(
        functools.partial(per_device, mesh.shape["pair"], mesh.shape["rep"]),
        mesh=mesh, in_specs=placed, out_specs=P(("pair", "rep"), None), check_vma=False
    )
```

time: 63.9 us -> 29.7 us (0.46)
  Pallas kernels: 0 us -> 25.3 us
  blocking collectives: 23.9 us -> 0 us
  waiting for transfers between devices: 21.2 us -> 0 us
  between operations: 13.4 us -> 0.01 us
  local copies, waits for them, and re-layouts: 1.56 us -> 4.11 us
  other arithmetic: 1.82 us -> 0 us
  matrix products: 1.78 us -> 0 us
    pallas_call x0 -> x1, Pallas kernels: none -> 25.3 us  [per_device(): pl.pallas_call(functools.partial(kernel, n, R), out_shape=jax.ShapeDtypeS...]
    reduce_scatter x1 -> x0, waiting for transfers between devices: 21.2 us -> none  [per_device(): ladder = lax.psum_scatter(regrouped, 'rep', scatter_dimension=0, tiled=True)]
    all_to_all x1 -> x0, blocking collectives: 12.3 us -> none  [per_device(): lax.all_to_all(partial_value, 'pair', split_axis=0, concat_axis=1, tiled=...]
    all_gather x1 -> x0, blocking collectives: 11.6 us -> none  [per_device(): lax.all_gather(amplitudes, 'pair', axis=0, tiled=True)]
    unnamed x4 -> x11, local copies, waits for them, and re-layouts: 0.01 us -> 4.11 us
    dot_general x1 -> x0, matrix products: 1.78 us -> none  [per_device(): jnp.dot(lax.all_gather(amplitudes, 'pair', axis=0, tiled=True), masked, p...]
    div x1 -> x0, other arithmetic: 1.65 us -> none  [per_device(): return ladder / (vir_energy[None, :] - occ_energy[:, None])]
    all_to_all x1 -> x0, local copies, waits for them, and re-layouts: 0.83 us -> none  [per_device(): lax.all_to_all(partial_value, 'pair', split_axis=0, concat_axis=1, tiled=...]
  transfers between devices with their start and end apart: 1 -> 0, of which waited for: 1 -> 0; matrix products, arithmetic and copies ran while one was open for 0% -> 0% of each run, Pallas kernels for 0% -> 0%
where the time goes in v1:
time: 29.7 us; the launch traced here: 29.4 us
  Pallas kernels  25.3 us (85%)
  local copies, waits for them, and re-layouts  4.11 us (14%)
    pallas_call x1, Pallas kernels, per_device(): pl.pallas_call(functools.partial(kernel, n, R), out_shape=jax.ShapeDtypeS...  25.3 us
    unnamed x11, local copies, waits for them, and re-layouts  4.11 us

profile of v1, /device:TPU:0, one launch (start us, length us, event | category | flops | bytes accessed | tf_op | source)
XLA Modules:
  0.0 29.4 jit_solution(7788212401107033449)
XLA Ops:
  0.0 0.0 copy-start.4
  0.0 0.0 copy-start.3
  0.0 0.7 %copy-done.4 = f32[8]{0:T(128)S(1)} copy-done((f32[8]{0:T(128)S(1)}, f32[8]{0:T(128)}, u32[]{:S(2)}) %copy-start.4) | copy-done | bytes 56
  0.7 0.0 copy-done.3
  0.7 0.0 copy-start
  0.7 1.2 %copy-done = bf16[1024,512]{1,0:T(8,128)(2,1)S(1)} copy-done((bf16[1024,512]{1,0:T(8,128)(2,1)S(1)}, bf16[1024,512]{1,0:T(8,128)(2,1)}, u32[]{:S(2)}) %copy-start) | copy-done | bytes 1048600
  1.9 0.0 copy-start.1
  1.9 0.8 %copy-done.1 = bf16[32,1024]{1,0:T(8,128)(2,1)S(1)} copy-done((bf16[32,1024]{1,0:T(8,128)(2,1)S(1)}, bf16[32,1024]{1,0:T(8,128)(2,1)}, u32[]{:S(2)}) %copy-start.1) | copy-done | bytes 65560
  2.7 0.0 copy-start.2
  2.7 0.7 %copy-done.2 = f32[4096]{0:T(1024)S(1)} copy-done((f32[4096]{0:T(1024)S(1)}, f32[4096]{0:T(1024)}, u32[]{:S(2)}) %copy-start.2) | copy-done | bytes 16408
  3.5 25.3 %shard_map.55 = f32[8,4096]{1,0:T(8,128)S(1)} custom-call(bf16[32,1024]{1,0:T(8,128)(2,1)S(1)} %copy-done.1, bf16[1024,512]{1,0:T(8,128)(2,1)S(1)} %copy-done, s32[9]{0:T(128)S(1)} %copy-done.3, f32[1,4096]{1,0:T(1,128)S(1)} %bitcast.1, f32[8]{0:T(128)S(1)} %copy-done.4), custom_call_target="tpu_custom_call" | custom-call | flops 268435456 | bytes 1048576 | tf_op jit(solution)/shard_map/pallas_call | solution.py:167
  28.8 0.7 %copy.7 = f32[8,4096]{1,0:T(8,128)} copy(f32[8,4096]{1,0:T(8,128)S(1)} %shard_map.55) | data formatting | bytes 262144
Async XLA Ops:
  0.0 0.7 %copy-start.4 = (f32[8]{0:T(128)S(1)}, f32[8]{0:T(128)}, u32[]{:S(2)}) copy-start(f32[8]{0:T(128)} %occ_ref.1) | copy-start | bytes 100
  0.0 0.7 %copy-start.3 = (s32[9]{0:T(128)S(1)}, s32[9]{0:T(128)}, u32[]{:S(2)}) copy-start(s32[9]{0:T(128)} %off_ref.1) | copy-start | bytes 112
  0.7 1.2 %copy-start = (bf16[1024,512]{1,0:T(8,128)(2,1)S(1)}, bf16[1024,512]{1,0:T(8,128)(2,1)}, u32[]{:S(2)}) copy-start(bf16[1024,512]{1,0:T(8,128)(2,1)} %int_ref.1) | copy-start | bytes 3145732
  1.9 0.8 %copy-start.1 = (bf16[32,1024]{1,0:T(8,128)(2,1)S(1)}, bf16[32,1024]{1,0:T(8,128)(2,1)}, u32[]{:S(2)}) copy-start(bf16[32,1024]{1,0:T(8,128)(2,1)} %amp_ref.1) | copy-start | bytes 196612
  2.7 0.7 %copy-start.2 = (f32[4096]{0:T(1024)S(1)}, f32[4096]{0:T(1024)}, u32[]{:S(2)}) copy-start(f32[4096]{0:T(1024)} %param.8) | copy-start | bytes 49156

commit v2 on v1

--- a/solution.py
+++ b/solution.py
@@ -11,8 +11,8 @@
 MESH = pl.DeviceIdType.MESH
 
 
-def kernel(n, R, amp_ref, int_ref, off_ref, ve_ref, occ_ref, out_ref,
-           amp_all, masked, part, rs_buf, red, fin,
+def kernel(n, R, amp_ref, int_ref, off_hbm, ve_hbm, occ_hbm, out_ref,
+           amp_all, masked, part, rs_buf, red, fin, ve_ref, off_ref, occ_ref,
            load_sem, ag_send, ag_recv, rs_send, rs_recv, fin_send, fin_recv):
     p = lax.axis_index("pair")
     r = lax.axis_index("rep")
@@ -42,9 +42,17 @@
     for i in range(1, R):
         pl.semaphore_signal(barrier, inc=1, device_id=(p, (r + i) % R), device_id_type=MESH)
 
-    load = pltpu.make_async_copy(int_ref, masked, load_sem)
+    offsets_load = pltpu.make_async_copy(off_hbm, off_ref, load_sem.at[0])
+    load = pltpu.make_async_copy(int_ref, masked, load_sem.at[1])
+    own_load = pltpu.make_async_copy(amp_ref, amp_all.at[p], load_sem.at[2])
+    virtual_load = pltpu.make_async_copy(ve_hbm, ve_ref, load_sem.at[3])
+    occupied_load = pltpu.make_async_copy(occ_hbm, occ_ref, load_sem.at[4])
+    offsets_load.start()
     load.start()
-    amp_all[p] = amp_ref[...]
+    own_load.start()
+    virtual_load.start()
+    occupied_load.start()
+    offsets_load.wait()
 
     col = lax.broadcasted_iota(jnp.int32, (8, cols), 1) + p * cols
     lo = jnp.zeros((8, cols), jnp.int32)
@@ -55,6 +63,23 @@
         hi = jnp.where(col < edge, jnp.minimum(hi, edge), hi)
     lo = lo[:1] - r * K
     hi = hi[:1] - r * K
+    pl.semaphore_wait(barrier, n - 1 + R - 1)
+
+    def gather_copy(to):
+        return pltpu.make_async_remote_copy(
+            src_ref=amp_ref, dst_ref=amp_all.at[p], send_sem=ag_send.at[to], recv_sem=ag_recv.at[p],
+            device_id=(to, r), device_id_type=MESH)
+
+    def gather_from(q):
+        return pltpu.make_async_remote_copy(
+            src_ref=amp_ref, dst_ref=amp_all.at[q], send_sem=ag_send.at[q], recv_sem=ag_recv.at[q],
+            device_id=(q, r), device_id_type=MESH)
+
+    def send_amp(t, c):
+        gather_copy(peer(t, -1)).start()
+        return c
+    lax.fori_loop(1, n, send_amp, 0)
+
     load.wait()
 
     step = 128
@@ -68,22 +93,7 @@
         return c
     lax.fori_loop(0, K // step, mask_rows, 0)
 
-    pl.semaphore_wait(barrier, n - 1 + R - 1)
-
-    def gather_copy(to):
-        return pltpu.make_async_remote_copy(
-            src_ref=amp_ref, dst_ref=amp_all.at[p], send_sem=ag_send.at[to], recv_sem=ag_recv.at[p],
-            device_id=(to, r), device_id_type=MESH)
-
-    def gather_from(q):
-        return pltpu.make_async_remote_copy(
-            src_ref=amp_ref, dst_ref=amp_all.at[q], send_sem=ag_send.at[q], recv_sem=ag_recv.at[q],
-            device_id=(q, r), device_id_type=MESH)
-
-    def send_amp(t, c):
-        gather_copy(peer(t, -1)).start()
-        return c
-    lax.fori_loop(1, n, send_amp, 0)
+    own_load.wait()
 
     def sum_copy(q, to, slot):
         return pltpu.make_async_remote_copy(
@@ -128,6 +138,8 @@
         return c
     lax.fori_loop(0, n, reduce, 0)
 
+    virtual_load.wait()
+    occupied_load.wait()
     which = lax.broadcasted_iota(jnp.int32, (m, cols), 0)
     occ = jnp.zeros((m, cols), jnp.float32)
     for i in range(m):
@@ -162,12 +174,11 @@
     cols = integrals.shape[1]
     m = rows // R
     vmem = pl.BlockSpec(memory_space=pltpu.VMEM)
-    smem = pl.BlockSpec(memory_space=pltpu.SMEM)
     dma = pltpu.SemaphoreType.DMA
     return pl.pallas_call(
         functools.partial(kernel, n, R),
         out_shape=jax.ShapeDtypeStruct((m, n * cols), jnp.float32),
-        in_specs=[vmem, pl.BlockSpec(memory_space=pl.ANY), smem, vmem, smem],
+        in_specs=[pl.BlockSpec(memory_space=pltpu.HBM)] * 5,
         out_specs=vmem,
         scratch_shapes=[
             pltpu.VMEM((n, rows, K), jnp.bfloat16),
@@ -176,10 +187,13 @@
             pltpu.VMEM((n, R, m, cols), jnp.float32),
             pltpu.VMEM((n, m, cols), jnp.float32),
             pltpu.VMEM((n, m, cols), jnp.float32),
-            dma, dma((n,)), dma((n,)), dma((n, R)), dma((n, R)), dma((n,)), dma((n,)),
+            pltpu.VMEM((1, n * cols), jnp.float32),
+            pltpu.SMEM(vir_offsets.shape, jnp.int32),
+            pltpu.SMEM(occ_energy.shape, jnp.float32),
+            dma((5,)), dma((n,)), dma((n,)), dma((n, R)), dma((n, R)), dma((n,)), dma((n,)),
         ],
         compiler_params=pltpu.CompilerParams(
-            collective_id=0, has_side_effects=True, vmem_limit_bytes=40 * 1024 * 1024),
+            collective_id=0, has_side_effects=True, vmem_limit_bytes=56 * 1024 * 1024),
         cost_estimate=pl.CostEstimate(
             flops=2 * n * rows * K * cols, bytes_accessed=2 * K * cols, transcendentals=0),
     )(amplitudes, integrals, vir_offsets, vir_energy.reshape(1, -1), occ_energy)

time: 29.7 us -> 27.1 us (0.912)
  local copies, waits for them, and re-layouts: 4.11 us -> 1.57 us
    unnamed x11 -> x1, local copies, waits for them, and re-layouts: 4.11 us -> 1.57 us
where the time goes in v2:
time: 27.1 us; the launch traced here: 27 us
  Pallas kernels  25.4 us (94%)
  local copies, waits for them, and re-layouts  1.57 us (6%)
    pallas_call x1, Pallas kernels, per_device(): pl.pallas_call(functools.partial(kernel, n, R), out_shape=jax.ShapeDtypeS...  25.4 us
    unnamed x1, local copies, waits for them, and re-layouts  1.57 us

profile of v2, /device:TPU:0, one launch (start us, length us, event | category | flops | bytes accessed | tf_op | source)
XLA Modules:
  0.0 27.0 jit_solution(7528408836386330052)
XLA Ops:
  0.0 25.4 %shard_map.55 = f32[8,4096]{1,0:T(8,128)} custom-call(bf16[32,1024]{1,0:T(8,128)(2,1)} %amp_ref.1, bf16[1024,512]{1,0:T(8,128)(2,1)} %int_ref.1, s32[9]{0:T(128)} %off_hbm.1, f32[1,4096]{1,0:T(1,128)} %bitcast.1, f32[8]{0:T(128)} %occ_hbm.1), custom_call_target="tpu_custom_call" | custom-call | flops 268435456 | bytes 1048576 | tf_op jit(solution)/shard_map/pallas_call | solution.py:178
  25.4 1.6 %copy.7 = f32[8,4096]{1,0:T(8,128)} copy(f32[8,4096]{1,0:T(8,128)} %shard_map.55) | data formatting | bytes 262144

commit v3 on v2

--- a/solution.py
+++ b/solution.py
@@ -100,6 +100,42 @@
             src_ref=part.at[q, to], dst_ref=rs_buf.at[q, slot], send_sem=rs_send.at[q, to],
             recv_sem=rs_recv.at[q, slot], device_id=(p, to), device_id_type=MESH)
 
+    fold = R == 4
+    other = r + 1 - 2 * (r % 2)
+    near = 2 - r // 2
+    far = 3 - 3 * (r // 2)
+    inner = (r + 1) // 2 == 1
+
+    def fold_copy(q, piece, slot, to):
+        return pltpu.make_async_remote_copy(
+            src_ref=part.at[q, piece], dst_ref=rs_buf.at[q, slot], send_sem=rs_send.at[q, piece],
+            recv_sem=rs_recv.at[q, slot], device_id=(p, to), device_id_type=MESH)
+
+    def fold_start(q):
+        @pl.when(inner)
+        def _():
+            fold_copy(q, other, 0, other).start()
+
+        @pl.when(jnp.logical_not(inner))
+        def _():
+            fold_copy(q, far, 3, other).start()
+            fold_copy(q, near, 2, other).start()
+            fold_copy(q, other, 0, other).start()
+
+    def relay(t):
+        q = peer(t, 1)
+
+        @pl.when(inner)
+        def _():
+            fold_copy(q, far, 3, far).wait_recv()
+            part[q, far] = part[q, far] + rs_buf[q, 3]
+            fold_copy(q, far, 1, far).start()
+            fold_copy(q, near, 2, near).wait_recv()
+            part[q, near] = part[q, near] + rs_buf[q, 2]
+            fold_copy(q, near, 1, near).start()
+
+    lag = 2
+
     def multiply(t, c):
         q = peer(t, 1)
 
@@ -109,8 +145,15 @@
         d = jnp.dot(amp_all[q], masked[...], preferred_element_type=jnp.float32)
         for k in range(R):
             part[q, k] = d[k * m:(k + 1) * m]
-        for i in range(1, R):
-            sum_copy(q, (r + i) % R, r).start()
+        if fold:
+            fold_start(q)
+
+            @pl.when(t >= lag)
+            def _():
+                relay(t - lag)
+        else:
+            for i in range(1, R):
+                sum_copy(q, (r + i) % R, r).start()
         return c
     lax.fori_loop(0, n, multiply, 0)
 
@@ -122,10 +165,18 @@
     def reduce(t, c):
         q = peer(t, 1)
         total = part[q, r]
-        for i in range(1, R):
-            k = (r + i) % R
-            sum_copy(q, k, k).wait_recv()
-            total = total + rs_buf[q, k]
+        if fold:
+            @pl.when(t < lag)
+            def _():
+                relay(n - lag + t)
+            for slot in range(2):
+                fold_copy(q, other, slot, other).wait_recv()
+                total = total + rs_buf[q, slot]
+        else:
+            for i in range(1, R):
+                k = (r + i) % R
+                sum_copy(q, k, k).wait_recv()
+                total = total + rs_buf[q, k]
 
         @pl.when(t == 0)
         def _():

time: 27.1 us -> 27.2 us (level)
  no operation moved by 1% of the time
where the time goes in v3:
time: 27.2 us; the launch traced here: 27 us
  Pallas kernels  25.4 us (93%)
  local copies, waits for them, and re-layouts  1.57 us (6%)
    pallas_call x1, Pallas kernels, per_device(): pl.pallas_call(functools.partial(kernel, n, R), out_shape=jax.ShapeDtypeS...  25.4 us
    unnamed x1, local copies, waits for them, and re-layouts  1.57 us

profile of v3, /device:TPU:0, one launch (start us, length us, event | category | flops | bytes accessed | tf_op | source)
XLA Modules:
  0.0 27.0 jit_solution(12124188859876654750)
XLA Ops:
  0.0 25.4 %shard_map.55 = f32[8,4096]{1,0:T(8,128)} custom-call(bf16[32,1024]{1,0:T(8,128)(2,1)} %amp_ref.1, bf16[1024,512]{1,0:T(8,128)(2,1)} %int_ref.1, s32[9]{0:T(128)} %off_hbm.1, f32[1,4096]{1,0:T(1,128)} %bitcast.1, f32[8]{0:T(128)} %occ_hbm.1), custom_call_target="tpu_custom_call" | custom-call | flops 268435456 | bytes 1048576 | tf_op jit(solution)/shard_map/pallas_call | solution.py:229
  25.5 1.6 %copy.7 = f32[8,4096]{1,0:T(8,128)} copy(f32[8,4096]{1,0:T(8,128)} %shard_map.55) | data formatting | bytes 262144

commit v4 on v3

--- a/solution.py
+++ b/solution.py
@@ -27,11 +27,13 @@
     cy = p // 2 // X
 
     def peer(t, sign):
-        s = t + 1
-        o = s // 2
+        other_core = t // chips
+        o = t - other_core * (chips - 1)
         x = (cx + X + sign * (o % X)) % X
         y = (cy + 2 * Y + sign * (o // X)) % Y
-        return (y * X + x) * 2 + (core + (s + 1) % 2) % 2
+        return (y * X + x) * 2 + (core + other_core) % 2
+
+    sibling = p + 1 - 2 * core
 
     barrier = pltpu.get_barrier_semaphore()
 
@@ -78,7 +80,13 @@
     def send_amp(t, c):
         gather_copy(peer(t, -1)).start()
         return c
-    lax.fori_loop(1, n, send_amp, 0)
+    lax.fori_loop(1, chips, send_amp, 0)
+    gather_copy(sibling).start()
+
+    def pass_on(q):
+        return pltpu.make_async_remote_copy(
+            src_ref=amp_all.at[q], dst_ref=amp_all.at[q], send_sem=ag_send.at[q + 1 - 2 * core],
+            recv_sem=ag_recv.at[q], device_id=(sibling, r), device_id_type=MESH)
 
     load.wait()
 
@@ -142,6 +150,10 @@
         @pl.when(t > 0)
         def _():
             gather_from(q).wait_recv()
+
+        @pl.when((t > 0) & (t < chips))
+        def _():
+            pass_on(q).start()
         d = jnp.dot(amp_all[q], masked[...], preferred_element_type=jnp.float32)
         for k in range(R):
             part[q, k] = d[k * m:(k + 1) * m]

time: 27.2 us -> 26.8 us (0.985)
  the two profiles are of different devices: /device:TPU:0 before, /device:TPU:1 now
where the time goes in v4:
time: 26.8 us; the launch traced here: 26.6 us
  Pallas kernels  25 us (93%)
  local copies, waits for them, and re-layouts  1.57 us (6%)
    pallas_call x1, Pallas kernels, per_device(): pl.pallas_call(functools.partial(kernel, n, R), out_shape=jax.ShapeDtypeS...  25 us
    unnamed x1, local copies, waits for them, and re-layouts  1.57 us

profile of v4, /device:TPU:1, one launch (start us, length us, event | category | flops | bytes accessed | tf_op | source)
XLA Modules:
  0.0 26.6 jit_solution(8599459422505495262)
XLA Ops:
  0.0 25.0 %shard_map.55 = f32[8,4096]{1,0:T(8,128)} custom-call(bf16[32,1024]{1,0:T(8,128)(2,1)} %amp_ref.1, bf16[1024,512]{1,0:T(8,128)(2,1)} %int_ref.1, s32[9]{0:T(128)} %off_hbm.1, f32[1,4096]{1,0:T(1,128)} %bitcast.1, f32[8]{0:T(128)} %occ_hbm.1), custom_call_target="tpu_custom_call" | custom-call | flops 268435456 | bytes 1048576 | tf_op jit(solution)/shard_map/pallas_call | solution.py:241
  25.1 1.6 %copy.7 = f32[8,4096]{1,0:T(8,128)} copy(f32[8,4096]{1,0:T(8,128)} %shard_map.55) | data formatting | bytes 262144

commit v5 on v2

--- a/solution.py
+++ b/solution.py
@@ -27,11 +27,13 @@
     cy = p // 2 // X
 
     def peer(t, sign):
-        s = t + 1
-        o = s // 2
+        other_core = t // chips
+        o = t - other_core * (chips - 1)
         x = (cx + X + sign * (o % X)) % X
         y = (cy + 2 * Y + sign * (o // X)) % Y
-        return (y * X + x) * 2 + (core + (s + 1) % 2) % 2
+        return (y * X + x) * 2 + (core + other_core) % 2
+
+    sibling = p + 1 - 2 * core
 
     barrier = pltpu.get_barrier_semaphore()
 
@@ -78,7 +80,13 @@
     def send_amp(t, c):
         gather_copy(peer(t, -1)).start()
         return c
-    lax.fori_loop(1, n, send_amp, 0)
+    lax.fori_loop(1, chips, send_amp, 0)
+    gather_copy(sibling).start()
+
+    def pass_on(q):
+        return pltpu.make_async_remote_copy(
+            src_ref=amp_all.at[q], dst_ref=amp_all.at[q], send_sem=ag_send.at[q + 1 - 2 * core],
+            recv_sem=ag_recv.at[q], device_id=(sibling, r), device_id_type=MESH)
 
     load.wait()
 
@@ -106,13 +114,16 @@
         @pl.when(t > 0)
         def _():
             gather_from(q).wait_recv()
+
+        @pl.when((t > 0) & (t < chips))
+        def _():
+            pass_on(q).start()
         d = jnp.dot(amp_all[q], masked[...], preferred_element_type=jnp.float32)
         for k in range(R):
             part[q, k] = d[k * m:(k + 1) * m]
         for i in range(1, R):
             sum_copy(q, (r + i) % R, r).start()
         return c
-    lax.fori_loop(0, n, multiply, 0)
 
     def final_copy(to, slot):
         return pltpu.make_async_remote_copy(
@@ -136,7 +147,18 @@
             red[q] = total
             final_copy(q, p).start()
         return c
-    lax.fori_loop(0, n, reduce, 0)
+    behind = 3
+
+    def advance(t, c):
+        @pl.when(t < n)
+        def _():
+            multiply(t, c)
+
+        @pl.when(t >= behind)
+        def _():
+            reduce(t - behind, c)
+        return c
+    lax.fori_loop(0, n + behind, advance, 0)
 
     virtual_load.wait()
     occupied_load.wait()

time: 27.1 us -> 25.9 us (0.956)
  the two profiles are of different devices: /device:TPU:0 before, /device:TPU:1 now
where the time goes in v5:
time: 25.9 us; the launch traced here: 25.7 us
  Pallas kernels  24.1 us (93%)
  local copies, waits for them, and re-layouts  1.57 us (6%)
    pallas_call x1, Pallas kernels, per_device(): pl.pallas_call(functools.partial(kernel, n, R), out_shape=jax.ShapeDtypeS...  24.1 us
    unnamed x1, local copies, waits for them, and re-layouts  1.57 us

profile of v5, /device:TPU:1, one launch (start us, length us, event | category | flops | bytes accessed | tf_op | source)
XLA Modules:
  0.0 25.7 jit_solution(5884905592063914211)
XLA Ops:
  0.0 24.1 %shard_map.55 = f32[8,4096]{1,0:T(8,128)} custom-call(bf16[32,1024]{1,0:T(8,128)(2,1)} %amp_ref.1, bf16[1024,512]{1,0:T(8,128)(2,1)} %int_ref.1, s32[9]{0:T(128)} %off_hbm.1, f32[1,4096]{1,0:T(1,128)} %bitcast.1, f32[8]{0:T(128)} %occ_hbm.1), custom_call_target="tpu_custom_call" | custom-call | flops 268435456 | bytes 1048576 | tf_op jit(solution)/shard_map/pallas_call | solution.py:200
  24.1 1.6 %copy.7 = f32[8,4096]{1,0:T(8,128)} copy(f32[8,4096]{1,0:T(8,128)} %shard_map.55) | data formatting | bytes 262144

commit v6 on v5

--- a/solution.py
+++ b/solution.py
@@ -12,7 +12,7 @@
 
 
 def kernel(n, R, amp_ref, int_ref, off_hbm, ve_hbm, occ_hbm, out_ref,
-           amp_all, masked, part, rs_buf, red, fin, ve_ref, off_ref, occ_ref,
+           amp_all, masked, part, rs_buf, red, fin, ve_ref, off_ref, occ_ref, out_buf, out_sem,
            load_sem, ag_send, ag_recv, rs_send, rs_recv, fin_send, fin_recv):
     p = lax.axis_index("pair")
     r = lax.axis_index("rep")
@@ -167,6 +167,10 @@
     for i in range(m):
         occ = jnp.where(which == i, occ_ref[i], occ)
 
+    def write_out(q):
+        at = pl.ds(pl.multiple_of(q * cols, cols), cols)
+        return pltpu.make_async_copy(out_buf.at[:, at], out_ref.at[:, at], out_sem.at[q])
+
     def finish(t, c):
         q = peer(t, 1)
 
@@ -174,12 +178,14 @@
         def _():
             final_copy(q, q).wait_recv()
         at = pl.ds(pl.multiple_of(q * cols, cols), cols)
-        out_ref[:, at] = fin[q] / (ve_ref[:, at] - occ)
+        out_buf[:, at] = fin[q] / (ve_ref[:, at] - occ)
+        write_out(q).start()
         return c
     lax.fori_loop(0, n, finish, 0)
 
     def drain(t, c):
         q = peer(t, 1)
+        write_out(q).wait()
 
         @pl.when(t > 0)
         def _():
@@ -195,13 +201,12 @@
     rows, K = amplitudes.shape
     cols = integrals.shape[1]
     m = rows // R
-    vmem = pl.BlockSpec(memory_space=pltpu.VMEM)
     dma = pltpu.SemaphoreType.DMA
     return pl.pallas_call(
         functools.partial(kernel, n, R),
         out_shape=jax.ShapeDtypeStruct((m, n * cols), jnp.float32),
         in_specs=[pl.BlockSpec(memory_space=pltpu.HBM)] * 5,
-        out_specs=vmem,
+        out_specs=pl.BlockSpec(memory_space=pltpu.HBM),
         scratch_shapes=[
             pltpu.VMEM((n, rows, K), jnp.bfloat16),
             pltpu.VMEM((K, cols), jnp.bfloat16),
@@ -212,6 +217,8 @@
             pltpu.VMEM((1, n * cols), jnp.float32),
             pltpu.SMEM(vir_offsets.shape, jnp.int32),
             pltpu.SMEM(occ_energy.shape, jnp.float32),
+            pltpu.VMEM((m, n * cols), jnp.float32),
+            dma((n,)),
             dma((5,)), dma((n,)), dma((n,)), dma((n, R)), dma((n, R)), dma((n,)), dma((n,)),
         ],
         compiler_params=pltpu.CompilerParams(

time: 25.9 us -> 25.6 us (0.988)
  Pallas kernels: 24.1 us -> 23.8 us
    pallas_call x1, Pallas kernels: 24.1 us -> 23.8 us  [per_device(): pl.pallas_call(functools.partial(kernel, n, R), out_shape=jax.ShapeDtypeS...]
where the time goes in v6:
time: 25.6 us; the launch traced here: 25.4 us
  Pallas kernels  23.8 us (93%)
  local copies, waits for them, and re-layouts  1.57 us (6%)
    pallas_call x1, Pallas kernels, per_device(): pl.pallas_call(functools.partial(kernel, n, R), out_shape=jax.ShapeDtypeS...  23.8 us
    unnamed x1, local copies, waits for them, and re-layouts  1.57 us

profile of v6, /device:TPU:1, one launch (start us, length us, event | category | flops | bytes accessed | tf_op | source)
XLA Modules:
  0.0 25.4 jit_solution(16457752181023543637)
XLA Ops:
  0.0 23.8 %shard_map.55 = f32[8,4096]{1,0:T(8,128)} custom-call(bf16[32,1024]{1,0:T(8,128)(2,1)} %amp_ref.1, bf16[1024,512]{1,0:T(8,128)(2,1)} %int_ref.1, s32[9]{0:T(128)} %off_hbm.1, f32[1,4096]{1,0:T(1,128)} %bitcast.1, f32[8]{0:T(128)} %occ_hbm.1), custom_call_target="tpu_custom_call" | custom-call | flops 268435456 | bytes 1048576 | tf_op jit(solution)/shard_map/pallas_call | solution.py:205
  23.8 1.6 %copy.7 = f32[8,4096]{1,0:T(8,128)} copy(f32[8,4096]{1,0:T(8,128)} %shard_map.55) | data formatting | bytes 262144

commit v7 on v6

--- a/solution.py
+++ b/solution.py
@@ -167,6 +167,17 @@
     for i in range(m):
         occ = jnp.where(which == i, occ_ref[i], occ)
 
+    def drain_early(t, c):
+        q = peer(t, 1)
+
+        @pl.when(t > 0)
+        def _():
+            gather_from(q).wait_send()
+        for i in range(1, R):
+            sum_copy(q, (r + i) % R, r).wait_send()
+        return c
+    lax.fori_loop(0, n, drain_early, 0)
+
     def write_out(q):
         at = pl.ds(pl.multiple_of(q * cols, cols), cols)
         return pltpu.make_async_copy(out_buf.at[:, at], out_ref.at[:, at], out_sem.at[q])
@@ -189,10 +200,7 @@
 
         @pl.when(t > 0)
         def _():
-            gather_from(q).wait_send()
             final_copy(q, p).wait_send()
-        for i in range(1, R):
-            sum_copy(q, (r + i) % R, r).wait_send()
         return c
     lax.fori_loop(0, n, drain, 0)
 

time: 25.6 us -> 25.6 us (level)
  no operation moved by 1% of the time
where the time goes in v7:
time: 25.6 us; the launch traced here: 25.4 us
  Pallas kernels  23.8 us (93%)
  local copies, waits for them, and re-layouts  1.57 us (6%)
    pallas_call x1, Pallas kernels, per_device(): pl.pallas_call(functools.partial(kernel, n, R), out_shape=jax.ShapeDtypeS...  23.8 us
    unnamed x1, local copies, waits for them, and re-layouts  1.57 us

profile of v7, /device:TPU:1, one launch (start us, length us, event | category | flops | bytes accessed | tf_op | source)
XLA Modules:
  0.0 25.4 jit_solution(15850684518748090451)
XLA Ops:
  0.0 23.8 %shard_map.55 = f32[8,4096]{1,0:T(8,128)} custom-call(bf16[32,1024]{1,0:T(8,128)(2,1)} %amp_ref.1, bf16[1024,512]{1,0:T(8,128)(2,1)} %int_ref.1, s32[9]{0:T(128)} %off_hbm.1, f32[1,4096]{1,0:T(1,128)} %bitcast.1, f32[8]{0:T(128)} %occ_hbm.1), custom_call_target="tpu_custom_call" | custom-call | flops 268435456 | bytes 1048576 | tf_op jit(solution)/shard_map/pallas_call | solution.py:213
  23.8 1.6 %copy.7 = f32[8,4096]{1,0:T(8,128)} copy(f32[8,4096]{1,0:T(8,128)} %shard_map.55) | data formatting | bytes 262144
